TPU v7x, 128 devices: a whole 4x4x4 slice. The times are simulated.
128 devices in a mesh: seq: 16 (over z, y), expert: 8 (over x, core).
Axes of the slice: x: 4, y: 4, z: 4, core: 2. Of those that a mesh axis runs over, the one named last changes fastest.
Arguments:
- tokens: bfloat16 [2048, 4096], P(('seq', 'expert')), may hold values from -6 to 6
- gain_mamba: float32 [4096], replicated, may hold values from 0.1 to 1.9
- in_weight: bfloat16 [2, 4096, 8192], P(None, 'seq', 'expert'), may hold values from -0.09375 to 0.09375
- conv_weight: float32 [4, 8192], P(None, 'expert'), may hold values from -3 to 3
- conv_bias: float32 [8192], P('expert'), may hold values from -3 to 3
- xproj_weight: bfloat16 [8192, 288], P('expert'), may hold values from -0.0625 to 0.0625
- dt_weight: bfloat16 [256, 8192], P(None, 'expert'), may hold values from -0.375 to 0.375
- dt_bias: float32 [8192], P('expert'), may hold values from -7 to -2
- a_rate: float32 [16, 8192], P(None, 'expert'), may hold values from 0.01 to 8
- skip_d: float32 [8192], P('expert'), may hold values from 0.5 to 1.5
- out_weight: bfloat16 [8192, 4096], P('expert', 'seq'), may hold values from -0.0625 to 0.0625
- gain_moe: float32 [4096], replicated, may hold values from 0.1 to 1.9
- expert_ids: int32 [2048, 2], P(('seq', 'expert')), may hold values from 0 to 15, all different within a row; in each aligned block of 16 rows (0 to 15, 16 to 31, ...) at most 4 rows name the same one
- gate_weights: float32 [2048, 2], P(('seq', 'expert')), may hold values from 0.2 to 1
- w_gate: bfloat16 [16, 4096, 7168], P('seq', None, 'expert'), may hold values from -0.09375 to 0.09375
- w_up: bfloat16 [16, 4096, 7168], P('seq', None, 'expert'), may hold values from -0.09375 to 0.09375
- w_down: bfloat16 [16, 7168, 4096], P('seq', 'expert'), may hold values from -0.0625 to 0.0625
Outputs:
- mixed: bfloat16 [2048, 4096], P(('seq', 'expert'))
Inputs may be any that keep to these rules, and one draw needn't show every extreme that they name: `expert_ids`: each row names 2 different experts. In each aligned block of 16 rows (the rows of one device) no expert is named by more than 4 rows, a bound that some block reaches.
All inputs are finite; a program needn't handle non-finite values.
Results may differ from a plain program's by a relative error of at most 0.03.
Values may be sent and summed in bfloat16 or wider, within the bound.
A program may use at most 192 MiB of HBM per device.

v0:
```python
import jax
import jax.numpy as jnp
from jax import lax
from jax.sharding import PartitionSpec as P

STATE = 16
CONV = 4
RANK = 256
TOP = 2


def from_behind(block, axis, distance):
    devices = range(lax.axis_size(axis))
    route = [(i - distance, i) for i in devices if i - distance in devices]
    return lax.ppermute(block, axis, route)


def rms_norm(values, gain):
    wide = values.astype(jnp.float32)
    return wide * lax.rsqrt(jnp.mean(wide * wide, axis=-1, keepdims=True) + 1e-05) * gain


def combine_states(earlier, later):
    return (earlier[0] * later[0], later[0] * earlier[1] + later[1])


def per_device(
    tokens,
    gain_mamba,
    in_weight,
    conv_weight,
    conv_bias,
    xproj_weight,
    dt_weight,
    dt_bias,
    a_rate,
    skip_d,
    out_weight,
    gain_moe,
    expert_ids,
    gate_weights,
    w_gate,
    w_up,
    w_down,
):
    rows, dim = tokens.shape
    n_seq = lax.axis_size("seq")
    n_exp = lax.axis_size("expert")
    group = lax.all_gather(tokens, "expert", axis=0, tiled=True)
    local_tok = group.shape[0]
    normed = rms_norm(group, gain_mamba).astype(jnp.bfloat16)
    both = jnp.einsum(
        "td,kdc->tkc",
        normed,
        lax.all_gather(in_weight, "seq", axis=1, tiled=True),
        preferred_element_type=jnp.float32,
    )
    xpart = both[:, 0]
    zpart = both[:, 1]
    edge = from_behind(xpart[local_tok - (CONV - 1) :], "seq", 1)
    padded = jnp.concatenate([edge, xpart], axis=0)
    conv = conv_bias
    for tap in range(CONV):
        conv = conv + conv_weight[tap] * padded[tap : tap + local_tok]
    inner = jax.nn.silu(conv).astype(jnp.bfloat16)
    partial_value = jnp.dot(inner, xproj_weight, preferred_element_type=jnp.float32)
    low_part, edge_part = (
        lax.psum(partial_value[:, :RANK].astype(jnp.bfloat16), "expert").astype(jnp.float32),
        lax.psum(partial_value[:, RANK:].astype(jnp.bfloat16), "expert").astype(jnp.float32),
    )
    dt_low = low_part.astype(jnp.bfloat16)
    bmat = edge_part[:, :STATE]
    cmat = edge_part[:, STATE:]
    step = jax.nn.softplus(jnp.dot(dt_low, dt_weight, preferred_element_type=jnp.float32) + dt_bias)
    inner_f = inner.astype(jnp.float32)
    decay = jnp.exp(-step[:, None, :] * a_rate[None, :, :])
    source = bmat[:, :, None] * (step * inner_f)[:, None, :]
    cumulative, states = lax.associative_scan(combine_states, (decay, source), axis=0)
    total = cumulative[-1]
    final = states[-1]

    def relay(turn, incoming):
        return from_behind((total * incoming + final).astype(jnp.bfloat16), "seq", 1).astype(
            jnp.float32
        )

    arriving = lax.fori_loop(0, n_seq - 1, relay, jnp.zeros_like(final))
    states = states + cumulative * arriving[None, :, :]
    readout = jnp.sum(cmat[:, :, None] * states, axis=1)
    gated = ((readout + skip_d * inner_f) * jax.nn.silu(zpart)).astype(jnp.bfloat16)
    terms = jnp.dot(
        gated,
        lax.all_gather(out_weight, "seq", axis=1, tiled=True),
        preferred_element_type=jnp.float32,
    )
    mixer = lax.psum_scatter(
        terms.astype(jnp.bfloat16), "expert", scatter_dimension=0, tiled=True
    ).astype(jnp.float32)
    resid = (tokens.astype(jnp.float32) + mixer).astype(jnp.bfloat16)
    normed2 = rms_norm(resid, gain_moe).astype(jnp.bfloat16)
    capacity = max(2, 4 * rows // n_seq)
    slots_all = n_seq * capacity
    flat_ids = expert_ids.reshape(-1)
    onehot = (flat_ids[:, None] == jnp.arange(n_seq, dtype=jnp.int32)[None, :]).astype(jnp.int32)
    before = jnp.cumsum(onehot, axis=0) - onehot
    slot = jnp.sum(before * onehot, axis=1)
    target = flat_ids * capacity + slot
    places = target[:, None] == jnp.arange(slots_all, dtype=jnp.int32)[None, :]
    dispatch_mat = jnp.any(places.reshape(rows, TOP, slots_all), axis=1).astype(jnp.bfloat16)
    send = jnp.einsum(
        "rp,rd->pd", dispatch_mat, normed2, preferred_element_type=jnp.float32
    ).astype(jnp.bfloat16)
    received = lax.all_to_all(
        send.reshape(n_seq, capacity, dim), "seq", split_axis=0, concat_axis=0, tiled=True
    )
    pooled = lax.all_gather(
        received.reshape(1, slots_all, dim), "expert", axis=0, tiled=True
    ).reshape(n_exp * slots_all, dim)
    gate = jnp.dot(pooled, w_gate[0], preferred_element_type=jnp.float32)
    upper = jnp.dot(pooled, w_up[0], preferred_element_type=jnp.float32)
    act = (jax.nn.silu(gate) * upper).astype(jnp.bfloat16)
    outputs = lax.psum_scatter(
        jnp.dot(act, w_down[0], preferred_element_type=jnp.float32).astype(jnp.bfloat16),
        "expert",
        scatter_dimension=0,
        tiled=True,
    )
    returned = lax.all_to_all(
        outputs.reshape(n_seq, capacity, dim), "seq", split_axis=0, concat_axis=0, tiled=True
    ).reshape(slots_all, dim)
    weighting = jnp.where(places, gate_weights.reshape(-1)[:, None], 0.0)
    weighting = jnp.sum(weighting.reshape(rows, TOP, slots_all), axis=1)
    moe = jnp.dot(weighting, returned.astype(jnp.float32), precision=lax.Precision.HIGHEST)
    return (resid.astype(jnp.float32) + moe).astype(jnp.bfloat16)


def solution(mesh):
    placed = (
        P(("seq", "expert"), None),
        P(),
        P(None, "seq", "expert"),
        P(None, "expert"),
        P("expert"),
        P("expert", None),
        P(None, "expert"),
        P("expert"),
        P(None, "expert"),
        P("expert"),
        P("expert", "seq"),
        P(),
        P(("seq", "expert"), None),
        P(("seq", "expert"), None),
        P("seq", None, "expert"),
        P("seq", None, "expert"),
        P("seq", "expert", None),
    )
    return jax.shard_map(
        per_device,
        mesh=mesh,
        in_specs=placed,
        out_specs=P(("seq", "expert"), None),
        check_vma=False,
    )
```

profile of v0, /device:TPU:0, one launch (start us, length us, event | category | flops | bytes accessed | tf_op | source)
XLA Modules:
  0.0 908.5 jit_solution(7577490913799089768)
XLA Ops:
  8.9 26.0 %all-gather.5.cloned.1.call-done = bf16[128,4096]{1,0:T(8,128)(2,1)} async-done(((bf16[16,4096]{1,0:T(8,128)(2,1)}), bf16[128,4096]{1,0:T(8,128)(2,1)}) %all-gather.5.cloned.1.call-update) | async-done | bytes 1048592 | tf_op jit(solution)/shard_map/all_gather | solution.py:49
  36.5 111.9 %all-gather.7.cloned.1.call-done = bf16[2,4096,1024]{2,1,0:T(8,128)(2,1)} async-done(((bf16[2,256,1024]{2,1,0:T(8,128)(2,1)}), bf16[2,4096,1024]{2,1,0:T(8,128)(2,1)}) %all-gather.7.cloned.1.call-update) | async-done | bytes 16777232 | tf_op jit(solution)/shard_map/all_gather | solution.py:55
  163.9 14.0 %psum.14 = bf16[128,32]{0,1:T(8,128)(2,1)S(1)} all-reduce(bf16[128,32]{0,1:T(8,128)(2,1)S(1)} %slice.341), channel_id=1, replica_groups=mesh['seq'=16,'expert'=8] {'expert'}, use_global_device_ids=true, to_apply=%region_1.2 | all-reduce | flops 4096 | bytes 16384 | tf_op jit(solution)/shard_map/psum | solution.py:69
  178.7 44.8 %all-reduce.30.cloned.1.call-done = bf16[128,256]{0,1:T(8,128)(2,1)} async-done(((bf16[128,256]{0,1:T(8,128)(2,1)}), bf16[128,256]{0,1:T(8,128)(2,1)}) %all-reduce.30.cloned.1.call-update) | async-done | bytes 65552 | tf_op jit(solution)/shard_map/psum | solution.py:68
  233.5 10.9 %slice_add_fusion = (f32[64,16,1024]{2,1,0:T(8,128)S(1)}, f32[64,16,1024]{2,1,0:T(8,128)}) fusion(f32[128,16,1024]{2,1,0:T(8,128)} %copy-done.3, f32[128,16,1024]{2,1,0:T(8,128)} %copy-done.2), kind=kLoop, calls=%fused_computation.19 | loop fusion | flops 3145728 | bytes 25165824 | tf_op jit(solution)/shard_map/add | solution.py:24
  315.3 10.2 %pad.109 = f32[32,16,1024]{2,1,0:T(8,128)} pad(f32[16,16,1024]{2,1,0:T(8,128)} %add.263, f32[]{:T(128)} %constant.13.clone.1), padding=1_0_1x0_0_0x0_0_0 | pad | bytes 3145732 | tf_op jit(solution)/shard_map/pad | solution.py:78
  325.5 10.1 %pad.95 = f32[32,16,1024]{2,1,0:T(8,128)} pad(f32[16,16,1024]{2,1,0:T(8,128)} %add.253, f32[]{:T(128)} %constant.13.clone.1), padding=1_0_1x0_0_0x0_0_0 | pad | bytes 3145732 | tf_op jit(solution)/shard_map/pad | solution.py:78
  337.9 10.2 %pad.94 = f32[32,16,1024]{2,1,0:T(8,128)} pad(f32[16,16,1024]{2,1,0:T(8,128)} %pad_maximum_fusion.4, f32[]{:T(128)} %constant.13.clone.1), padding=0_1_1x0_0_0x0_0_0 | pad | bytes 3145732 | tf_op jit(solution)/shard_map/pad | solution.py:78
  362.0 18.6 %pad.96 = f32[64,16,1024]{2,1,0:T(8,128)} pad(f32[32,16,1024]{2,1,0:T(8,128)} %pad_maximum_fusion.2, f32[]{:T(128)} %constant.13.clone.1), padding=0_1_1x0_0_0x0_0_0 | pad | bytes 6291460 | tf_op jit(solution)/shard_map/pad | solution.py:78
  380.6 12.0 %pad.97 = f32[64,16,1024]{2,1,0:T(8,128)} pad(f32[32,16,1024]{2,1,0:T(8,128)S(1)} %copy-done.16, f32[]{:T(128)} %constant.13.clone.1), padding=1_0_1x0_0_0x0_0_0 | pad | bytes 6291460 | tf_op jit(solution)/shard_map/pad | solution.py:78
  399.4 35.6 %pad.99 = f32[128,16,1024]{2,1,0:T(8,128)} pad(f32[64,16,1024]{2,1,0:T(8,128)} %add.257, f32[]{:T(128)} %constant.13.clone.1), padding=1_0_1x0_0_0x0_0_0 | pad | bytes 12582916 | tf_op jit(solution)/shard_map/pad | solution.py:78
  436.5 18.6 %pad.110 = f32[64,16,1024]{2,1,0:T(8,128)} pad(f32[32,16,1024]{2,1,0:T(8,128)} %pad_maximum_fusion.3, f32[]{:T(128)} %constant.13.clone.1), padding=0_1_1x0_0_0x0_0_0 | pad | bytes 6291460 | tf_op jit(solution)/shard_map/pad | solution.py:78
  455.1 11.9 %pad.111 = f32[64,16,1024]{2,1,0:T(8,128)} pad(f32[32,16,1024]{2,1,0:T(8,128)S(1)} %copy-done.15, f32[]{:T(128)} %constant.13.clone.1), padding=1_0_1x0_0_0x0_0_0 | pad | bytes 6291460 | tf_op jit(solution)/shard_map/pad | solution.py:78
  485.7 35.5 %pad.98 = f32[128,16,1024]{2,1,0:T(8,128)} pad(f32[64,16,1024]{2,1,0:T(8,128)} %pad_maximum_fusion, f32[]{:T(128)} %constant.13.clone.1), padding=0_1_1x0_0_0x0_0_0 | pad | bytes 12582916 | tf_op jit(solution)/shard_map/pad | solution.py:78
  521.2 35.5 %pad.113 = f32[128,16,1024]{2,1,0:T(8,128)} pad(f32[64,16,1024]{2,1,0:T(8,128)} %add.265, f32[]{:T(128)} %constant.13.clone.1), padding=1_0_1x0_0_0x0_0_0 | pad | bytes 12582916 | tf_op jit(solution)/shard_map/pad | solution.py:78
  561.5 35.5 %pad.112 = f32[128,16,1024]{2,1,0:T(8,128)} pad(f32[64,16,1024]{2,1,0:T(8,128)} %pad_maximum_fusion.1, f32[]{:T(128)} %constant.13.clone.1), padding=0_1_1x0_0_0x0_0_0 | pad | bytes 12582916 | tf_op jit(solution)/shard_map/pad | solution.py:78
  598.8 107.7 %while.11 = (s32[]{:T(128)}, f32[16,1024]{1,0:T(8,128)S(1)}, f32[16,1024]{1,0:T(8,128)S(1)}, f32[16,1024]{1,0:T(8,128)S(1)}, s32[]{:T(128)}, /*index=5*/s32[]{:T(128)}) while((s32[]{:T(128)}, f32[16,1024]{1,0:T(8,128)S(1)}, f32[16,1024]{1,0:T(8,128)S(1)}, f32[16,1024]{1,0:T(8,128)S(1)}, s32[]{:T(128)}, /*index=5*/s32[]{:T(128)}) %tuple.47), condition=%wide.region_4.5_spmd.clone, body=%wide.region_3.4_spmd.clone.sunk | while | flops 81923 | bytes 458871 | solution.py:87
  706.5 14.0 %multiply_reduce_fusion = f32[128,1024]{1,0:T(8,128)S(1)} fusion(f32[128,16,1024]{2,1,0:T(8,128)} %pad.112, f32[128,16,1024]{2,1,0:T(8,128)} %pad.113, f32[128,16,1024]{2,1,0:T(8,128)} %pad.98, f32[128,16,1024]{2,1,0:T(8,128)} %pad.99, f32[16,1024]{1,0:T(8,128)S(1)} %get-tuple-element.27, f32[128,16]{1,0:T(8,128)S(1)} %copy-done.28), kind=kLoop, calls=%fused_computation.3 | loop fusion | flops 12451840 | bytes 34152448 | tf_op jit(solution)/shard_map/reduce_sum | solution.py:89
  727.1 39.7 %reduce-scatter.3.cloned.1.call-done = bf16[16,4096]{1,0:T(8,128)(2,1)} async-done(((bf16[128,4096]{1,0:T(8,128)(2,1)}), bf16[16,4096]{1,0:T(8,128)(2,1)}) %reduce-scatter.3.cloned.1.call-update) | async-done | bytes 131088 | tf_op jit(solution)/shard_map/reduce_scatter | solution.py:96
  769.3 16.9 %all_to_all.10 = bf16[16,4,4096]{2,1,0:T(4,128)(2,1)S(1)} all-to-all(bf16[16,4,4096]{2,1,0:T(4,128)(2,1)S(1)} %reshape.78), channel_id=1, replica_groups=mesh['seq'=16,'expert'=8] {'seq'}, dimensions={0} | all-to-all | bytes 1048576 | tf_op jit(solution)/shard_map/all_to_all | solution.py:113
  787.2 29.3 %all-gather.11.cloned.1.call-done = bf16[8,64,4096]{2,1,0:T(8,128)(2,1)} async-done(((bf16[1,64,4096]{2,1,0:T(8,128)(2,1)}), bf16[8,64,4096]{2,1,0:T(8,128)(2,1)}) %all-gather.11.cloned.1.call-update) | async-done | bytes 4194320 | tf_op jit(solution)/shard_map/all_gather | solution.py:116
  816.5 10.1 %fusion.6 = f32[512,896]{1,0:T(8,128)} fusion(bf16[512,4096]{1,0:T(8,128)(2,1)} %bitcast.51, bf16[1,4096,896]{2,1,0:T(8,128)(2,1)} %param.33), kind=kOutput, calls=%fused_computation.9 | convolution fusion | flops 3758096384 | bytes 13369344 | tf_op jit(solution)/shard_map/dot_general | solution.py:119
  826.6 16.7 %fusion.8 = bf16[512,4096]{1,0:T(8,128)(2,1)} fusion(bf16[1,896,4096]{2,1,0:T(8,128)(2,1)} %param.35, f32[512,896]{1,0:T(8,128)} %fusion.6, bf16[512,4096]{1,0:T(8,128)(2,1)} %bitcast.52, bf16[1,4096,896]{2,1,0:T(8,128)(2,1)} %param.34), kind=kOutput, calls=%fused_computation.11 | convolution fusion | flops 7521042432 | bytes 24903680 | tf_op jit(solution)/shard_map/dot_general | solution.py:123
  843.3 38.0 %reduce-scatter.5.cloned.1.call-done = bf16[64,4096]{1,0:T(8,128)(2,1)} async-done(((bf16[512,4096]{1,0:T(8,128)(2,1)}), bf16[64,4096]{1,0:T(8,128)(2,1)}) %reduce-scatter.5.cloned.1.call-update) | async-done | bytes 524304 | tf_op jit(solution)/shard_map/reduce_scatter | solution.py:122
  (265 shorter events, 288.3 us)
Async XLA Ops:
  6.5 28.4 %all-gather.5.cloned.1.call-start = ((), (), s32[]{:S(2)}) async-start(), calls=%async_computation.4 | async-start | bytes 1179648 | tf_op jit(solution)/shard_map/all_gather | solution.py:49
  7.3 141.1 %all-gather.7.cloned.1.call-start = ((), (), s32[]{:S(2)}) async-start(), calls=%async_computation.5 | async-start | bytes 17825792 | tf_op jit(solution)/shard_map/all_gather | solution.py:55
  8.0 215.6 %all-reduce.30.cloned.1.call-start = ((), (), s32[]{:S(2)}) async-start(), calls=%async_computation.6 | async-start | bytes 131072 | tf_op jit(solution)/shard_map/psum | solution.py:68
  156.9 5.0 collective-permute-start.1
  163.2 557.3 %all-gather.9.cloned.1.call-start = ((), (), s32[]{:S(2)}) async-start(), calls=%async_computation.7 | async-start | bytes 8912896 | tf_op jit(solution)/shard_map/all_gather | solution.py:93
  163.8 602.9 %reduce-scatter.3.cloned.1.call-start = ((), (), s32[]{:S(2)}) async-start(), calls=%async_computation.8 | async-start | bytes 1179648 | tf_op jit(solution)/shard_map/reduce_scatter | solution.py:96
  598.8 5.0 collective-permute-start
  603.9 5.8 collective-permute-start
  609.7 5.9 collective-permute-start
  615.6 5.8 collective-permute-start
  621.5 5.8 collective-permute-start
  627.3 7.2 collective-permute-start
  634.5 8.1 collective-permute-start
  642.6 8.1 collective-permute-start
  650.7 7.9 collective-permute-start
  658.6 7.9 collective-permute-start
  666.6 8.0 collective-permute-start
  674.6 7.8 collective-permute-start
  682.5 7.9 collective-permute-start
  690.4 8.1 collective-permute-start
  698.5 7.9 collective-permute-start
  726.3 90.2 %all-gather.11.cloned.1.call-start = ((), (), s32[]{:S(2)}) async-start(), calls=%async_computation.9 | async-start | bytes 4718592 | tf_op jit(solution)/shard_map/all_gather | solution.py:116
  787.1 94.2 %reduce-scatter.5.cloned.1.call-start = ((), (), s32[]{:S(2)}) async-start(), calls=%async_computation.10 | async-start | bytes 4718592 | tf_op jit(solution)/shard_map/reduce_scatter | solution.py:122
  883.3 17.2 %all-to-all-start.1 = ((bf16[16,4,4096]{2,1,0:T(4,128)(2,1)}), bf16[16,4,4096]{2,1,0:T(4,128)(2,1)S(1)}, u32[]{:S(2)}, u32[]{:S(2)}) async-start(bf16[16,4,4096]{2,1,0:T(4,128)(2,1)} %reshape.81), calls=%async_computation.3 | async-start | bytes 1048576 | tf_op jit(solution)/shard_map/all_to_all | solution.py:128
  (45 other events, 1531.7 us)
Sparse Core Ops, SparseCore 0:
  9.1 25.7 all-gather.4
  37.0 111.3 all-gather.6
  163.4 60.1 all-reduce.29
  225.7 77.5 all-gather.8
  726.4 40.3 reduce-scatter.2
  787.2 29.2 all-gather.10
  843.4 37.8 reduce-scatter.4
where the time goes:
time: 924 us; the launch traced here: 909 us
  waiting for transfers between devices  327 us (35%)
  local copies, waits for them, and re-layouts  289 us (31%)
  other arithmetic  109 us (12%)
  starting transfers between devices  94.2 us (10%)
  matrix products  44.8 us (5%)
  blocking collectives  30.9 us (3%)
  between operations  14 us (2%)
    pad x24, local copies, waits for them, and re-layouts, per_device(): lax.associative_scan(combine_states, (decay, source), axis=0)  267 us
    all_gather x1, waiting for transfers between devices, per_device(): lax.all_gather(in_weight, 'seq', axis=1, tiled=True)  112 us
    ppermute x16, starting transfers between devices, from_behind(): return lax.ppermute(block, axis, route)  86.9 us
    psum x1, waiting for transfers between devices, per_device(): lax.psum(partial_value[:, :RANK].astype(jnp.bfloat16), 'expert')  44.8 us
    reduce_scatter x1, waiting for transfers between devices, per_device(): lax.psum_scatter(terms.astype(jnp.bfloat16), 'expert', scatter_dimension=...  39.7 us
    reduce_scatter x1, waiting for transfers between devices, per_device(): lax.psum_scatter(jnp.dot(act, w_down[0], preferred_element_type=jnp.float...  38 us
    add x12, other arithmetic, combine_states(): return (earlier[0] * later[0], later[0] * earlier[1] + later[1])  34.6 us
    add x12, other arithmetic, per_device(): lax.associative_scan(combine_states, (decay, source), axis=0)  33.2 us
  transfers between devices with their start and end apart: 24, of which 23 were waited for; matrix products, arithmetic and copies ran while one was open for 42% of the time, Pallas kernels for 0%

commit v1 on v0

--- a/solution.py
+++ b/solution.py
@@ -65,7 +65,9 @@
     inner = jax.nn.silu(conv).astype(jnp.bfloat16)
     partial_value = jnp.dot(inner, xproj_weight, preferred_element_type=jnp.float32)
     low_part, edge_part = (
-        lax.psum(partial_value[:, :RANK].astype(jnp.bfloat16), "expert").astype(jnp.float32),
+        jnp.sum(
+            lax.all_gather(partial_value[:, :RANK].astype(jnp.bfloat16), "expert"), axis=0
+        ).astype(jnp.float32),
         lax.psum(partial_value[:, RANK:].astype(jnp.bfloat16), "expert").astype(jnp.float32),
     )
     dt_low = low_part.astype(jnp.bfloat16)

time: 924 us -> 894 us (0.968)
  waiting for transfers between devices: 327 us -> 282 us
  blocking collectives: 30.9 us -> 44.3 us
    psum x1 -> x0, waiting for transfers between devices: 44.8 us -> none  [per_device(): lax.psum(partial_value[:, :RANK].astype(jnp.bfloat16), 'expert')]
    all_gather x0 -> x1, blocking collectives: none -> 12.9 us  [per_device(): lax.all_gather(partial_value[:, :RANK].astype(jnp.bfloat16), 'expert')]
  transfers between devices with their start and end apart: 24 -> 23, of which waited for: 23 -> 22; matrix products, arithmetic and copies ran while one was open for 42% -> 45% of each run, Pallas kernels for 0% -> 0%
where the time goes in v1:
time: 894 us; the launch traced here: 878 us
  local copies, waits for them, and re-layouts  287 us (32%)
  waiting for transfers between devices  282 us (32%)
  other arithmetic  110 us (12%)
  starting transfers between devices  96.7 us (11%)
  blocking collectives  44.3 us (5%)
  matrix products  44.1 us (5%)
  between operations  14 us (2%)
    pad x24, local copies, waits for them, and re-layouts, per_device(): lax.associative_scan(combine_states, (decay, source), axis=0)  266 us
    all_gather x1, waiting for transfers between devices, per_device(): lax.all_gather(in_weight, 'seq', axis=1, tiled=True)  112 us
    ppermute x16, starting transfers between devices, from_behind(): return lax.ppermute(block, axis, route)  89.4 us
    reduce_scatter x1, waiting for transfers between devices, per_device(): lax.psum_scatter(terms.astype(jnp.bfloat16), 'expert', scatter_dimension=...  39.9 us
    reduce_scatter x1, waiting for transfers between devices, per_device(): lax.psum_scatter(jnp.dot(act, w_down[0], preferred_element_type=jnp.float...  37.9 us
    add x12, other arithmetic, combine_states(): return (earlier[0] * later[0], later[0] * earlier[1] + later[1])  34.5 us
    add x12, other arithmetic, per_device(): lax.associative_scan(combine_states, (decay, source), axis=0)  33.2 us
    all_gather x1, waiting for transfers between devices, per_device(): lax.all_gather(received.reshape(1, slots_all, dim), 'expert', axis=0, til...  29.3 us
  transfers between devices with their start and end apart: 23, of which 22 were waited for; matrix products, arithmetic and copies ran while one was open for 45% of the time, Pallas kernels for 0%

profile of v1, /device:TPU:0, one launch (start us, length us, event | category | flops | bytes accessed | tf_op | source)
XLA Modules:
  0.0 878.2 jit_solution(4939895551040621163)
XLA Ops:
  9.7 25.2 %all-gather.6.cloned.1.call-done = bf16[128,4096]{1,0:T(8,128)(2,1)} async-done(((bf16[16,4096]{1,0:T(8,128)(2,1)}), bf16[128,4096]{1,0:T(8,128)(2,1)}) %all-gather.6.cloned.1.call-update) | async-done | bytes 1048592 | tf_op jit(solution)/shard_map/all_gather | solution.py:49
  36.4 112.0 %all-gather.8.cloned.1.call-done = bf16[2,4096,1024]{2,1,0:T(8,128)(2,1)} async-done(((bf16[2,256,1024]{2,1,0:T(8,128)(2,1)}), bf16[2,4096,1024]{2,1,0:T(8,128)(2,1)}) %all-gather.8.cloned.1.call-update) | async-done | bytes 16777232 | tf_op jit(solution)/shard_map/all_gather | solution.py:55
  162.6 12.9 %all-gather = bf16[1024,256]{0,1:T(8,128)(2,1)S(1)} all-gather(bf16[128,256]{0,1:T(8,128)(2,1)S(1)} %slice.344), channel_id=2, replica_groups=mesh['seq'=16,'expert'=8] {'expert'}, dimensions={0}, use_global_device_ids=true | all-gather | bytes 589824 | tf_op jit(solution)/shard_map/all_gather | solution.py:69
  175.7 14.4 %psum.7 = bf16[128,32]{0,1:T(8,128)(2,1)S(1)} all-reduce(bf16[128,32]{0,1:T(8,128)(2,1)S(1)} %slice.341), channel_id=1, replica_groups=mesh['seq'=16,'expert'=8] {'expert'}, use_global_device_ids=true, to_apply=%region_1.2 | all-reduce | flops 4096 | bytes 16384 | tf_op jit(solution)/shard_map/psum | solution.py:71
  199.6 10.9 %slice_add_fusion = (f32[64,16,1024]{2,1,0:T(8,128)S(1)}, f32[64,16,1024]{2,1,0:T(8,128)}) fusion(f32[128,16,1024]{2,1,0:T(8,128)} %copy-done.3, f32[128,16,1024]{2,1,0:T(8,128)} %copy-done.2), kind=kLoop, calls=%fused_computation.19 | loop fusion | flops 3145728 | bytes 25165824 | tf_op jit(solution)/shard_map/add | solution.py:24
  282.0 10.2 %pad.109 = f32[32,16,1024]{2,1,0:T(8,128)} pad(f32[16,16,1024]{2,1,0:T(8,128)} %add.261, f32[]{:T(128)} %constant.15.clone.1), padding=1_0_1x0_0_0x0_0_0 | pad | bytes 3145732 | tf_op jit(solution)/shard_map/pad | solution.py:80
  292.2 10.1 %pad.95 = f32[32,16,1024]{2,1,0:T(8,128)} pad(f32[16,16,1024]{2,1,0:T(8,128)} %add.251, f32[]{:T(128)} %constant.15.clone.1), padding=1_0_1x0_0_0x0_0_0 | pad | bytes 3145732 | tf_op jit(solution)/shard_map/pad | solution.py:80
  304.6 10.1 %pad.94 = f32[32,16,1024]{2,1,0:T(8,128)} pad(f32[16,16,1024]{2,1,0:T(8,128)} %pad_maximum_fusion.4, f32[]{:T(128)} %constant.15.clone.1), padding=0_1_1x0_0_0x0_0_0 | pad | bytes 3145732 | tf_op jit(solution)/shard_map/pad | solution.py:80
  328.7 18.6 %pad.96 = f32[64,16,1024]{2,1,0:T(8,128)} pad(f32[32,16,1024]{2,1,0:T(8,128)} %pad_maximum_fusion.2, f32[]{:T(128)} %constant.15.clone.1), padding=0_1_1x0_0_0x0_0_0 | pad | bytes 6291460 | tf_op jit(solution)/shard_map/pad | solution.py:80
  347.2 12.0 %pad.97 = f32[64,16,1024]{2,1,0:T(8,128)} pad(f32[32,16,1024]{2,1,0:T(8,128)S(1)} %copy-done.16, f32[]{:T(128)} %constant.15.clone.1), padding=1_0_1x0_0_0x0_0_0 | pad | bytes 6291460 | tf_op jit(solution)/shard_map/pad | solution.py:80
  366.0 35.6 %pad.99 = f32[128,16,1024]{2,1,0:T(8,128)} pad(f32[64,16,1024]{2,1,0:T(8,128)} %add.255, f32[]{:T(128)} %constant.15.clone.1), padding=1_0_1x0_0_0x0_0_0 | pad | bytes 12582916 | tf_op jit(solution)/shard_map/pad | solution.py:80
  403.1 18.6 %pad.110 = f32[64,16,1024]{2,1,0:T(8,128)} pad(f32[32,16,1024]{2,1,0:T(8,128)} %pad_maximum_fusion.3, f32[]{:T(128)} %constant.15.clone.1), padding=0_1_1x0_0_0x0_0_0 | pad | bytes 6291460 | tf_op jit(solution)/shard_map/pad | solution.py:80
  421.7 12.0 %pad.111 = f32[64,16,1024]{2,1,0:T(8,128)} pad(f32[32,16,1024]{2,1,0:T(8,128)S(1)} %copy-done.15, f32[]{:T(128)} %constant.15.clone.1), padding=1_0_1x0_0_0x0_0_0 | pad | bytes 6291460 | tf_op jit(solution)/shard_map/pad | solution.py:80
  452.4 35.6 %pad.98 = f32[128,16,1024]{2,1,0:T(8,128)} pad(f32[64,16,1024]{2,1,0:T(8,128)} %pad_maximum_fusion, f32[]{:T(128)} %constant.15.clone.1), padding=0_1_1x0_0_0x0_0_0 | pad | bytes 12582916 | tf_op jit(solution)/shard_map/pad | solution.py:80
  488.0 35.5 %pad.113 = f32[128,16,1024]{2,1,0:T(8,128)} pad(f32[64,16,1024]{2,1,0:T(8,128)} %add.263, f32[]{:T(128)} %constant.15.clone.1), padding=1_0_1x0_0_0x0_0_0 | pad | bytes 12582916 | tf_op jit(solution)/shard_map/pad | solution.py:80
  528.3 35.4 %pad.112 = f32[128,16,1024]{2,1,0:T(8,128)} pad(f32[64,16,1024]{2,1,0:T(8,128)} %pad_maximum_fusion.1, f32[]{:T(128)} %constant.15.clone.1), padding=0_1_1x0_0_0x0_0_0 | pad | bytes 12582916 | tf_op jit(solution)/shard_map/pad | solution.py:80
  565.6 110.3 %while.11 = (s32[]{:T(128)}, f32[16,1024]{1,0:T(8,128)S(1)}, f32[16,1024]{1,0:T(8,128)S(1)}, f32[16,1024]{1,0:T(8,128)S(1)}, s32[]{:T(128)}, /*index=5*/s32[]{:T(128)}) while((s32[]{:T(128)}, f32[16,1024]{1,0:T(8,128)S(1)}, f32[16,1024]{1,0:T(8,128)S(1)}, f32[16,1024]{1,0:T(8,128)S(1)}, s32[]{:T(128)}, /*index=5*/s32[]{:T(128)}) %tuple.47), condition=%wide.region_4.5_spmd.clone, body=%wide.region_3.4_spmd.clone.sunk | while | flops 81923 | bytes 458871 | solution.py:89
  675.9 14.0 %multiply_reduce_fusion = f32[128,1024]{1,0:T(8,128)S(1)} fusion(f32[128,16,1024]{2,1,0:T(8,128)} %pad.112, f32[128,16,1024]{2,1,0:T(8,128)} %pad.113, f32[128,16,1024]{2,1,0:T(8,128)} %pad.98, f32[128,16,1024]{2,1,0:T(8,128)} %pad.99, f32[16,1024]{1,0:T(8,128)S(1)} %get-tuple-element.27, f32[128,16]{1,0:T(8,128)S(1)} %copy.42), kind=kLoop, calls=%fused_computation.3 | loop fusion | flops 12451840 | bytes 34152448 | tf_op jit(solution)/shard_map/reduce_sum | solution.py:91
  696.5 39.9 %reduce-scatter.3.cloned.1.call-done = bf16[16,4096]{1,0:T(8,128)(2,1)} async-done(((bf16[128,4096]{1,0:T(8,128)(2,1)}), bf16[16,4096]{1,0:T(8,128)(2,1)}) %reduce-scatter.3.cloned.1.call-update) | async-done | bytes 131088 | tf_op jit(solution)/shard_map/reduce_scatter | solution.py:98
  738.9 16.9 %all_to_all.10 = bf16[16,4,4096]{2,1,0:T(4,128)(2,1)S(1)} all-to-all(bf16[16,4,4096]{2,1,0:T(4,128)(2,1)S(1)} %reshape.78), channel_id=1, replica_groups=mesh['seq'=16,'expert'=8] {'seq'}, dimensions={0} | all-to-all | bytes 1048576 | tf_op jit(solution)/shard_map/all_to_all | solution.py:115
  756.8 29.3 %all-gather.12.cloned.1.call-done = bf16[8,64,4096]{2,1,0:T(8,128)(2,1)} async-done(((bf16[1,64,4096]{2,1,0:T(8,128)(2,1)}), bf16[8,64,4096]{2,1,0:T(8,128)(2,1)}) %all-gather.12.cloned.1.call-update) | async-done | bytes 4194320 | tf_op jit(solution)/shard_map/all_gather | solution.py:118
  786.2 10.1 %fusion.6 = f32[512,896]{1,0:T(8,128)} fusion(bf16[512,4096]{1,0:T(8,128)(2,1)} %bitcast.57, bf16[1,4096,896]{2,1,0:T(8,128)(2,1)} %param.33), kind=kOutput, calls=%fused_computation.9 | convolution fusion | flops 3758096384 | bytes 13369344 | tf_op jit(solution)/shard_map/dot_general | solution.py:121
  796.2 16.7 %fusion.8 = bf16[512,4096]{1,0:T(8,128)(2,1)} fusion(bf16[1,896,4096]{2,1,0:T(8,128)(2,1)} %param.35, f32[512,896]{1,0:T(8,128)} %fusion.6, bf16[512,4096]{1,0:T(8,128)(2,1)} %bitcast.58, bf16[1,4096,896]{2,1,0:T(8,128)(2,1)} %param.34), kind=kOutput, calls=%fused_computation.11 | convolution fusion | flops 7521042432 | bytes 24903680 | tf_op jit(solution)/shard_map/dot_general | solution.py:125
  812.9 37.9 %reduce-scatter.5.cloned.1.call-done = bf16[64,4096]{1,0:T(8,128)(2,1)} async-done(((bf16[512,4096]{1,0:T(8,128)(2,1)}), bf16[64,4096]{1,0:T(8,128)(2,1)}) %reduce-scatter.5.cloned.1.call-update) | async-done | bytes 524304 | tf_op jit(solution)/shard_map/reduce_scatter | solution.py:124
  (263 shorter events, 290.1 us)
Async XLA Ops:
  6.5 155.7 %copy-start = (bf16[1024,288]{0,1:T(8,128)(2,1)S(1)}, bf16[1024,288]{0,1:T(8,128)(2,1)}, u32[]{:S(2)}) copy-start(bf16[1024,288]{0,1:T(8,128)(2,1)} %param.24) | copy-start | bytes 1769476
  6.5 28.4 %all-gather.6.cloned.1.call-start = ((), (), s32[]{:S(2)}) async-start(), calls=%async_computation.4 | async-start | bytes 1179648 | tf_op jit(solution)/shard_map/all_gather | solution.py:49
  7.3 141.1 %all-gather.8.cloned.1.call-start = ((), (), s32[]{:S(2)}) async-start(), calls=%async_computation.5 | async-start | bytes 17825792 | tf_op jit(solution)/shard_map/all_gather | solution.py:55
  8.0 681.9 %all-gather.10.cloned.1.call-start = ((), (), s32[]{:S(2)}) async-start(), calls=%async_computation.6 | async-start | bytes 8912896 | tf_op jit(solution)/shard_map/all_gather | solution.py:95
  8.7 727.6 %reduce-scatter.3.cloned.1.call-start = ((), (), s32[]{:S(2)}) async-start(), calls=%async_computation.7 | async-start | bytes 1179648 | tf_op jit(solution)/shard_map/reduce_scatter | solution.py:98
  156.9 5.0 collective-permute-start.1
  565.6 6.1 collective-permute-start
  571.7 5.8 collective-permute-start
  577.5 6.0 collective-permute-start
  583.6 5.9 collective-permute-start
  589.5 6.9 collective-permute-start
  596.4 7.9 collective-permute-start
  604.4 8.0 collective-permute-start
  612.4 7.8 collective-permute-start
  620.3 7.9 collective-permute-start
  628.2 7.9 collective-permute-start
  636.1 7.9 collective-permute-start
  644.1 8.0 collective-permute-start
  652.1 7.9 collective-permute-start
  660.0 7.9 collective-permute-start
  667.9 7.9 collective-permute-start
  695.7 90.5 %all-gather.12.cloned.1.call-start = ((), (), s32[]{:S(2)}) async-start(), calls=%async_computation.8 | async-start | bytes 4718592 | tf_op jit(solution)/shard_map/all_gather | solution.py:118
  756.8 94.1 %reduce-scatter.5.cloned.1.call-start = ((), (), s32[]{:S(2)}) async-start(), calls=%async_computation.9 | async-start | bytes 4718592 | tf_op jit(solution)/shard_map/reduce_scatter | solution.py:124
  852.9 17.3 %all-to-all-start.1 = ((bf16[16,4,4096]{2,1,0:T(4,128)(2,1)}), bf16[16,4,4096]{2,1,0:T(4,128)(2,1)S(1)}, u32[]{:S(2)}, u32[]{:S(2)}) async-start(bf16[16,4,4096]{2,1,0:T(4,128)(2,1)} %reshape.81), calls=%async_computation.3 | async-start | bytes 1048576 | tf_op jit(solution)/shard_map/all_to_all | solution.py:130
  (43 other events, 863.9 us)
Sparse Core Ops, SparseCore 0:
  9.1 25.7 all-gather.5
  37.0 111.3 all-gather.7
  150.5 78.3 all-gather.9
  695.8 40.5 reduce-scatter.2
  756.9 29.1 all-gather.11
  813.1 37.7 reduce-scatter.4
